TPU v7x, 32 devices: a whole 2x2x4 slice. The times are simulated.
32 devices in a mesh: quad: 4 (over z), gy: 2 (over y), gx: 4 (over x, core).
Axes of the slice: x: 2, y: 2, z: 4, core: 2. Of those that a mesh axis runs over, the one named last changes fastest.
Arguments:
- modes_now: bfloat16 [1024, 16, 512], P('quad', 'gy', 'gx'), may hold values from -4 to 4
- basis_rows: bfloat16 [4096, 1024], P('quad'), may hold values from -0.25 to 0.25
- quad_weights: float32 [4096], P('quad'), may hold values from 0.2 to 2
- germ_nodes: float32 [4096, 8], P('quad'), may hold values from -1.5 to 1.5
- log_fields: float32 [8, 16, 512], P(None, 'gy', 'gx'), may hold values from -1 to 1
- reaction_rates: float32 [4096], P('quad'), may hold values from 0.08 to 0.32
Outputs:
- modes_next: float32 [1024, 16, 512], P('quad', 'gy', 'gx')
All inputs are finite; a program needn't handle non-finite values.
Results may differ from a plain program's by a relative error of at most 0.02.
Values may be sent and summed in bfloat16 or wider, within the bound.
A program may use at most 64 MiB of HBM per device.

v0:
```python
import jax
import jax.numpy as jnp
from jax import lax
from jax.sharding import PartitionSpec as P

time_step = 0.04


def with_halo(array, sides, width):
    for axis, dim in sides:
        peers, length = (lax.axis_size(axis), array.shape[dim])
        up = [(i, (i + 1) % peers) for i in range(peers - 1)]
        down = [(j, i) for i, j in up]
        last = lax.slice_in_dim(array, length - width, length, axis=dim)
        leading = lax.slice_in_dim(array, 0, width, axis=dim)
        before = lax.ppermute(last, axis, up)
        after = lax.ppermute(leading, axis, down)
        array = jnp.concatenate([before, array, after], axis=dim)
    return array


def neighbour(array, drow, dcol):
    return array[:, 1 + drow : array.shape[1] - 1 + drow, 1 + dcol : array.shape[2] - 1 + dcol]


def drive_with(field_ext, coeff_ext, rates, weights):
    center = neighbour(field_ext, 0, 0)
    coeff_mid = neighbour(coeff_ext, 0, 0)
    total = jnp.zeros_like(center)
    for drow, dcol in ((-1, 0), (1, 0), (0, -1), (0, 1)):
        total = total + (coeff_mid + neighbour(coeff_ext, drow, dcol)) * (
            neighbour(field_ext, drow, dcol) - center
        )
    total = total + rates[:, None, None] * (center - center * center * center)
    return (weights[:, None, None] * total).astype(jnp.bfloat16).reshape(center.shape[0], -1)


def rim_fields(field):
    return with_halo(field, (("gy", 1), ("gx", 2)), 1)


def body(modes_now, basis_rows, quad_weights, germ_nodes, log_fields, reaction_rates):
    k_local, rows_y, cols_x = modes_now.shape
    q_local, modes_total = basis_rows.shape
    log_ext = with_halo(log_fields, (("gy", 1), ("gx", 2)), 1)
    coeff_ext = jnp.exp(
        jnp.einsum("qj,jyx->qyx", germ_nodes, log_ext, precision=lax.Precision.HIGHEST)
    )

    def drive(field_ext):
        return drive_with(field_ext, coeff_ext, reaction_rates, quad_weights)

    current = modes_now.astype(jnp.float32)
    gathered = lax.all_gather(modes_now.reshape(k_local, -1), "quad", axis=0, tiled=True)
    field_zero = jnp.dot(basis_rows, gathered, preferred_element_type=jnp.float32)
    field_zero = rim_fields(field_zero.reshape(q_local, rows_y, cols_x))
    inner = gathered.reshape(modes_total, rows_y, cols_x)
    weighted_zero = drive(field_zero)
    partial_sum = lax.dot_general(
        basis_rows, weighted_zero, (((0,), (0,)), ((), ())), preferred_element_type=jnp.float32
    )
    summed = (
        lax.psum(partial_sum.astype(jnp.bfloat16), "quad")
        .astype(jnp.float32)
        .reshape(modes_total, rows_y, cols_x)
    )
    iterate_one = (inner.astype(jnp.float32) + time_step * summed).astype(jnp.bfloat16)
    flat = iterate_one.reshape(modes_total, -1)
    field_one = rim_fields(
        jnp.dot(basis_rows, flat, preferred_element_type=jnp.float32).reshape(
            q_local, rows_y, cols_x
        )
    )
    weighted = drive(field_one)
    second = (
        lax.psum_scatter(
            lax.dot_general(
                basis_rows, weighted, (((0,), (0,)), ((), ())), preferred_element_type=jnp.float32
            ).astype(jnp.bfloat16),
            "quad",
            scatter_dimension=0,
            tiled=True,
        )
        .astype(jnp.float32)
        .reshape(k_local, rows_y, cols_x)
    )
    return current + time_step * second


def solution(mesh):
    in_specs = (
        P("quad", "gy", "gx"),
        P("quad", None),
        P("quad"),
        P("quad", None),
        P(None, "gy", "gx"),
        P("quad"),
    )
    out_specs = P("quad", "gy", "gx")
    return jax.shard_map(body, mesh=mesh, in_specs=in_specs, out_specs=out_specs, check_vma=False)
```

profile of v0, /device:TPU:9, one launch (start us, length us, event | category | flops | bytes accessed | tf_op | source)
XLA Modules:
  0.0 280.8 jit_solution(7784622140114972990)
XLA Ops:
  6.5 2.1 copy.16
  8.6 0.0 all-gather.2.cloned.1.call-update
  8.6 0.0 all-reduce.2.cloned.1.call-start
  8.7 0.8 fusion.43
  9.5 3.1 %collective-permute-start = (f32[8,1,128]{2,0,1:T(8,128)S(1)}, f32[8,1,128]{2,0,1:T(8,128)S(1)}, u32[]{:S(2)}, u32[]{:S(2)}) collective-permute-start(f32[8,1,128]{2,0,1:T(8,128)S(1)} %copy.14), channel_id=1, source_target_pairs={{0,4},{1,5},{2,6},{3,7},{8,12},{9,13},{10,14},{11,15},{16,20},{17,... | collective-permute-start | bytes 12296 | tf_op jit(solution)/shard_map/ppermute | solution.py:16
  12.7 1.3 collective-permute-start.1
  14.0 0.0 collective-permute-done
  14.0 0.0 copy-start.2
  14.0 40.2 %all-gather.2.cloned.1.call-done = bf16[1024,1024]{1,0:T(8,128)(2,1)} async-done(((bf16[256,1024]{1,0:T(8,128)(2,1)}), bf16[1024,1024]{1,0:T(8,128)(2,1)}) %all-gather.2.cloned.1.call-update) | async-done | bytes 2097168 | tf_op jit(solution)/shard_map/all_gather | solution.py:54
  54.2 4.1 %fusion.44 = f32[1024,1024]{0,1:T(8,128)S(1)} fusion(bf16[1024,1024]{1,0:T(8,128)(2,1)S(1)} %copy-done, bf16[1024,1024]{1,0:T(8,128)(2,1)} %all-gather.2.cloned.1.call-done), kind=kOutput, calls=%fused_computation.82 | convolution fusion | flops 2147483648 | bytes 8388608 | tf_op jit(solution)/shard_map/dot_general | solution.py:55
  58.3 0.0 copy-start.3
  58.3 0.1 fusion.41
  58.4 3.1 %collective-permute-start.4 = (f32[1024,1,128]{0,2,1:T(8,128)S(1)}, f32[1024,1,128]{0,2,1:T(8,128)S(1)}, u32[]{:S(2)}, u32[]{:S(2)}) collective-permute-start(f32[1024,1,128]{0,2,1:T(8,128)S(1)} %get-tuple-element.11), channel_id=1, source_target_pairs={{0,4},{1,5},{2,6},{3,7},{8,12},{9,13},{10,14},{11,15},{16,20},{17,... | collective-permute-start | bytes 1572872 | tf_op jit(solution)/shard_map/ppermute | solution.py:16
  61.5 1.3 collective-permute-start.5
  62.8 0.1 fusion.42
  62.9 4.2 %collective-permute-start.2 = (f32[8,10,1]{2,0,1:T(8,128)S(1)}, f32[8,10,1]{2,0,1:T(8,128)S(1)}, u32[]{:S(2)}, u32[]{:S(2)}) collective-permute-start(f32[8,10,1]{2,0,1:T(8,128)S(1)} %get-tuple-element.13), channel_id=1, source_target_pairs={{0,1},{1,2},{2,3},{4,5},{5,6},{6,7},{8,9},{9,10},{10,11},{12,13},{... | collective-permute-start | bytes 968 | tf_op jit(solution)/shard_map/ppermute | solution.py:16
  67.1 1.9 collective-permute-start.3
  69.1 2.7 collective-permute-done.4
  71.7 3.9 %collective-permute-done.5 = f32[1024,1,128]{0,2,1:T(8,128)S(1)} collective-permute-done((f32[1024,1,128]{0,2,1:T(8,128)S(1)}, f32[1024,1,128]{0,2,1:T(8,128)S(1)}, u32[]{:S(2)}, u32[]{:S(2)}) %collective-permute-start.5) | collective-permute-done | bytes 524320 | tf_op jit(solution)/shard_map/ppermute | solution.py:17
  75.6 0.1 pad_maximum_fusion.21
  75.7 0.0 copy-start.4
  75.7 0.0 copy-start.5
  75.7 5.1 %collective-permute-start.6 = (f32[1024,10,1]{0,2,1:T(1,128)S(1)}, f32[1024,10,1]{0,2,1:T(1,128)S(1)}, u32[]{:S(2)}, u32[]{:S(2)}) collective-permute-start(f32[1024,10,1]{0,2,1:T(1,128)S(1)} %get-tuple-element.7), channel_id=1, source_target_pairs={{0,1},{1,2},{2,3},{4,5},{5,6},{6,7},{8,9},{9,10},{10,11},{12,13},{... | collective-permute-start | bytes 122888 | tf_op jit(solution)/shard_map/ppermute | solution.py:16
  80.8 1.9 collective-permute-start.7
  82.7 0.0 collective-permute-done.2
  82.8 5.2 %exponential_bitcast_fusion = f32[1024,10,130]{0,2,1:T(8,128)S(1)} fusion(f32[8,10,1]{2,0,1:T(8,128)S(1)} %collective-permute-done.3, f32[8,10,128]{2,0,1:T(8,128)S(1)} %constant_dynamic-update-slice_fusion, f32[8,10,1]{2,0,1:T(8,128)S(1)} %collective-permute-done.2, f32[1024,8]{0,1:T(8,128)S(1)} %copy-done.3), kind=kOutput, calls=%fused_computation.2 | convolution fusion | flops 127816000 | bytes 5399168 | tf_op jit(solution)/shard_map/qj,jyx->qyx/dot_general | solution.py:47
  88.0 5.2 %fusion.3 = bf16[1024,8,128]{0,2,1:T(8,128)(2,1)S(1)} fusion(f32[1024,8,128]{0,2,1:T(8,128)S(1)} %bitcast.29, f32[1024,10,1]{0,2,1:T(1,128)S(1)} %collective-permute-done.7, f32[1024,1,128]{0,2,1:T(8,128)S(1)} %collective-permute-done.5, f32[1024,1,128]{0,2,1:T(8,128)S(1)} %collective-permute-done.4, f32[1024,10,1]{0,2,1:T(1,128)S(1)} %collective-permute-done.6, ...), kind=kLoop, calls=%fused_computation.6 | loop fusion | flops 31457280 | bytes 28401664 | tf_op jit(solution)/shard_map/convert_element_type | solution.py:35
  93.2 3.7 %convert_bitcast_fusion.1 = bf16[1024,1024]{1,0:T(8,128)(2,1)} fusion(bf16[1024,1024]{0,1:T(8,128)(2,1)S(1)} %bitcast.35, bf16[1024,1024]{1,0:T(8,128)(2,1)S(1)} %copy-done), kind=kOutput, calls=%fused_computation.57 | convolution fusion | flops 2148532224 | bytes 6291456 | tf_op jit(solution)/shard_map/dot_general | solution.py:59
  97.0 0.0 all-reduce.2.cloned.1.call-update
  97.0 0.2 reduce-scatter.2.cloned.1.call-start
  97.2 84.7 %all-reduce.2.cloned.1.call-done = bf16[1024,1024]{1,0:T(8,128)(2,1)} async-done(((bf16[1024,1024]{1,0:T(8,128)(2,1)}), bf16[1024,1024]{1,0:T(8,128)(2,1)}) %all-reduce.2.cloned.1.call-update) | async-done | bytes 2097168 | tf_op jit(solution)/shard_map/psum | solution.py:63
  181.9 4.6 %fusion.30 = f32[1024,1024]{1,0:T(8,128)S(1)} fusion(bf16[1024,1024]{1,0:T(8,128)(2,1)S(1)} %copy-done, bf16[1024,1024]{1,0:T(8,128)(2,1)} %all-reduce.2.cloned.1.call-done, bf16[1024,1024]{1,0:T(8,128)(2,1)} %all-gather.2.cloned.1.call-done), kind=kOutput, calls=%fused_computation.54 | convolution fusion | flops 2152726528 | bytes 10485760 | tf_op jit(solution)/shard_map/dot_general | solution.py:70
  186.5 0.1 fusion.40
  186.6 3.1 %collective-permute-start.8 = (f32[1024,1,128]{0,2,1:T(8,128)S(1)}, f32[1024,1,128]{0,2,1:T(8,128)S(1)}, u32[]{:S(2)}, u32[]{:S(2)}) collective-permute-start(f32[1024,1,128]{0,2,1:T(8,128)S(1)} %get-tuple-element.9), channel_id=1, source_target_pairs={{0,4},{1,5},{2,6},{3,7},{8,12},{9,13},{10,14},{11,15},{16,20},{17,... | collective-permute-start | bytes 1572872 | tf_op jit(solution)/shard_map/ppermute | solution.py:16
  189.7 1.3 collective-permute-start.9
  191.0 9.0 %collective-permute-done.8 = f32[1024,1,128]{0,2,1:T(8,128)S(1)} collective-permute-done((f32[1024,1,128]{0,2,1:T(8,128)S(1)}, f32[1024,1,128]{0,2,1:T(8,128)S(1)}, u32[]{:S(2)}, u32[]{:S(2)}) %collective-permute-start.8) | collective-permute-done | bytes 524320 | tf_op jit(solution)/shard_map/ppermute | solution.py:16
  200.0 3.8 %collective-permute-done.9 = f32[1024,1,128]{0,2,1:T(8,128)S(1)} collective-permute-done((f32[1024,1,128]{0,2,1:T(8,128)S(1)}, f32[1024,1,128]{0,2,1:T(8,128)S(1)}, u32[]{:S(2)}, u32[]{:S(2)}) %collective-permute-start.9) | collective-permute-done | bytes 524320 | tf_op jit(solution)/shard_map/ppermute | solution.py:17
  203.9 0.1 pad_maximum_fusion.18
  203.9 5.1 %collective-permute-start.10 = (f32[1024,10,1]{0,2,1:T(1,128)S(1)}, f32[1024,10,1]{0,2,1:T(1,128)S(1)}, u32[]{:S(2)}, u32[]{:S(2)}) collective-permute-start(f32[1024,10,1]{0,2,1:T(1,128)S(1)} %get-tuple-element.5), channel_id=1, source_target_pairs={{0,1},{1,2},{2,3},{4,5},{5,6},{6,7},{8,9},{9,10},{10,11},{12,13},{... | collective-permute-start | bytes 122888 | tf_op jit(solution)/shard_map/ppermute | solution.py:16
  209.0 1.9 collective-permute-start.11
  211.0 3.4 %collective-permute-done.11 = f32[1024,10,1]{0,2,1:T(1,128)S(1)} collective-permute-done((f32[1024,10,1]{0,2,1:T(1,128)S(1)}, f32[1024,10,1]{0,2,1:T(1,128)S(1)}, u32[]{:S(2)}, u32[]{:S(2)}) %collective-permute-start.11) | collective-permute-done | bytes 40992 | tf_op jit(solution)/shard_map/ppermute | solution.py:17
  214.3 11.3 %fusion.7 = bf16[1024,8,128]{0,2,1:T(8,128)(2,1)S(1)} fusion(f32[1024,8,128]{0,2,1:T(8,128)S(1)} %bitcast.32, f32[1024,10,1]{0,2,1:T(1,128)S(1)} %collective-permute-done.11, f32[1024,1,128]{0,2,1:T(8,128)S(1)} %collective-permute-done.9, f32[1024,1,128]{0,2,1:T(8,128)S(1)} %collective-permute-done.8, f32[1024,10,1]{0,2,1:T(1,128)S(1)} %collective-permute-done.10, ...), kind=kLoop, calls=%fused_computation.10 | loop fusion | flops 31457280 | bytes 28401664 | tf_op jit(solution)/shard_map/convert_element_type | solution.py:35
  225.6 3.7 %convert_bitcast_fusion = bf16[1024,1024]{0,1:T(8,128)(2,1)} fusion(bf16[1024,1024]{0,1:T(8,128)(2,1)S(1)} %bitcast.34, bf16[1024,1024]{1,0:T(8,128)(2,1)S(1)} %copy-done), kind=kOutput, calls=%fused_computation.55 | convolution fusion | flops 2148532224 | bytes 6291456 | tf_op jit(solution)/shard_map/dot_general | solution.py:77
  229.3 0.0 reduce-scatter.2.cloned.1.call-update
  229.3 40.1 %reduce-scatter.2.cloned.1.call-done = bf16[256,1024]{0,1:T(8,128)(2,1)} async-done(((bf16[1024,1024]{0,1:T(8,128)(2,1)}), bf16[256,1024]{0,1:T(8,128)(2,1)}) %reduce-scatter.2.cloned.1.call-update) | async-done | bytes 524304 | tf_op jit(solution)/shard_map/reduce_scatter | solution.py:76
  269.4 1.1 convert_multiply_fusion
  270.6 1.3 copy.10
  271.9 2.4 convert_add_fusion
  (19 shorter events, 0.1 us)
Async XLA Ops:
  6.5 47.7 %copy-start = (bf16[1024,1024]{1,0:T(8,128)(2,1)S(1)}, bf16[1024,1024]{1,0:T(8,128)(2,1)}, u32[]{:S(2)}) copy-start(bf16[1024,1024]{1,0:T(8,128)(2,1)} %param.7) | copy-start | bytes 6291460
  6.5 47.7 %all-gather.2.cloned.1.call-start = ((), (), s32[]{:S(2)}) async-start(), calls=%async_computation.1 | async-start | bytes 2621440 | tf_op jit(solution)/shard_map/all_gather | solution.py:54
  8.6 173.2 %all-reduce.2.cloned.1.call-start = ((), (), s32[]{:S(2)}) async-start(), calls=%async_computation.2 | async-start | bytes 4194304 | tf_op jit(solution)/shard_map/psum | solution.py:63
  9.5 4.5 %collective-permute-start = (f32[8,1,128]{2,0,1:T(8,128)S(1)}, f32[8,1,128]{2,0,1:T(8,128)S(1)}, u32[]{:S(2)}, u32[]{:S(2)}) collective-permute-start(f32[8,1,128]{2,0,1:T(8,128)S(1)} %copy.14), channel_id=1, source_target_pairs={{0,4},{1,5},{2,6},{3,7},{8,12},{9,13},{10,14},{11,15},{16,20},{17,... | collective-permute-start | bytes 12296 | tf_op jit(solution)/shard_map/ppermute | solution.py:16
  12.7 50.1 %collective-permute-start.1 = (f32[8,1,128]{2,0,1:T(8,128)S(1)}, f32[8,1,128]{2,0,1:T(8,128)S(1)}, u32[]{:S(2)}, u32[]{:S(2)}) collective-permute-start(f32[8,1,128]{2,0,1:T(8,128)S(1)} %copy.15), channel_id=1, source_target_pairs={{4,0},{5,1},{6,2},{7,3},{12,8},{13,9},{14,10},{15,11},{20,16},{21,... | collective-permute-start | bytes 12296 | tf_op jit(solution)/shard_map/ppermute | solution.py:17
  14.0 48.8 %copy-start.2 = (f32[8,8,128]{2,1,0:T(8,128)S(1)}, f32[8,8,128]{2,1,0:T(8,128)}, u32[]{:S(2)}) copy-start(f32[8,8,128]{2,1,0:T(8,128)} %param.10) | copy-start | bytes 98308
  58.3 24.5 %copy-start.3 = (f32[1024,8]{0,1:T(8,128)S(1)}, f32[1024,8]{0,1:T(8,128)}, u32[]{:S(2)}) copy-start(f32[1024,8]{0,1:T(8,128)} %param.9) | copy-start | bytes 98308
  58.4 13.4 %collective-permute-start.4 = (f32[1024,1,128]{0,2,1:T(8,128)S(1)}, f32[1024,1,128]{0,2,1:T(8,128)S(1)}, u32[]{:S(2)}, u32[]{:S(2)}) collective-permute-start(f32[1024,1,128]{0,2,1:T(8,128)S(1)} %get-tuple-element.11), channel_id=1, source_target_pairs={{0,4},{1,5},{2,6},{3,7},{8,12},{9,13},{10,14},{11,15},{16,20},{17,... | collective-permute-start | bytes 1572872 | tf_op jit(solution)/shard_map/ppermute | solution.py:16
  61.5 14.1 %collective-permute-start.5 = (f32[1024,1,128]{0,2,1:T(8,128)S(1)}, f32[1024,1,128]{0,2,1:T(8,128)S(1)}, u32[]{:S(2)}, u32[]{:S(2)}) collective-permute-start(f32[1024,1,128]{0,2,1:T(8,128)S(1)} %get-tuple-element.12), channel_id=1, source_target_pairs={{4,0},{5,1},{6,2},{7,3},{12,8},{13,9},{14,10},{15,11},{20,16},{21,... | collective-permute-start | bytes 1572872 | tf_op jit(solution)/shard_map/ppermute | solution.py:17
  62.9 19.8 %collective-permute-start.2 = (f32[8,10,1]{2,0,1:T(8,128)S(1)}, f32[8,10,1]{2,0,1:T(8,128)S(1)}, u32[]{:S(2)}, u32[]{:S(2)}) collective-permute-start(f32[8,10,1]{2,0,1:T(8,128)S(1)} %get-tuple-element.13), channel_id=1, source_target_pairs={{0,1},{1,2},{2,3},{4,5},{5,6},{6,7},{8,9},{9,10},{10,11},{12,13},{... | collective-permute-start | bytes 968 | tf_op jit(solution)/shard_map/ppermute | solution.py:16
  67.1 15.6 %collective-permute-start.3 = (f32[8,10,1]{2,0,1:T(8,128)S(1)}, f32[8,10,1]{2,0,1:T(8,128)S(1)}, u32[]{:S(2)}, u32[]{:S(2)}) collective-permute-start(f32[8,10,1]{2,0,1:T(8,128)S(1)} %get-tuple-element.14), channel_id=1, source_target_pairs={{1,0},{2,1},{3,2},{5,4},{6,5},{7,6},{9,8},{10,9},{11,10},{13,12},{... | collective-permute-start | bytes 968 | tf_op jit(solution)/shard_map/ppermute | solution.py:17
  75.7 12.4 %copy-start.4 = (f32[1024]{0:T(1024)S(1)}, f32[1024]{0:T(1024)}, u32[]{:S(2)}) copy-start(f32[1024]{0:T(1024)} %param.11) | copy-start | bytes 12292
  75.7 12.4 %copy-start.5 = (f32[1024]{0:T(1024)S(1)}, f32[1024]{0:T(1024)}, u32[]{:S(2)}) copy-start(f32[1024]{0:T(1024)} %param.8) | copy-start | bytes 12292
  75.7 12.3 %collective-permute-start.6 = (f32[1024,10,1]{0,2,1:T(1,128)S(1)}, f32[1024,10,1]{0,2,1:T(1,128)S(1)}, u32[]{:S(2)}, u32[]{:S(2)}) collective-permute-start(f32[1024,10,1]{0,2,1:T(1,128)S(1)} %get-tuple-element.7), channel_id=1, source_target_pairs={{0,1},{1,2},{2,3},{4,5},{5,6},{6,7},{8,9},{9,10},{10,11},{12,13},{... | collective-permute-start | bytes 122888 | tf_op jit(solution)/shard_map/ppermute | solution.py:16
  80.8 7.2 %collective-permute-start.7 = (f32[1024,10,1]{0,2,1:T(1,128)S(1)}, f32[1024,10,1]{0,2,1:T(1,128)S(1)}, u32[]{:S(2)}, u32[]{:S(2)}) collective-permute-start(f32[1024,10,1]{0,2,1:T(1,128)S(1)} %get-tuple-element.8), channel_id=1, source_target_pairs={{1,0},{2,1},{3,2},{5,4},{6,5},{7,6},{9,8},{10,9},{11,10},{13,12},{... | collective-permute-start | bytes 122888 | tf_op jit(solution)/shard_map/ppermute | solution.py:17
  88.0 5.2 %copy-start.1 = (f32[1024,10,130]{0,2,1:T(8,128)}, f32[1024,10,130]{0,2,1:T(8,128)S(1)}, u32[]{:S(2)}) copy-start(f32[1024,10,130]{0,2,1:T(8,128)S(1)} %exponential_bitcast_fusion) | copy-start | bytes 15974404
  97.0 172.4 %reduce-scatter.2.cloned.1.call-start = ((), (), s32[]{:S(2)}) async-start(), calls=%async_computation.3 | async-start | bytes 2621440 | tf_op jit(solution)/shard_map/reduce_scatter | solution.py:76
  186.6 13.4 %collective-permute-start.8 = (f32[1024,1,128]{0,2,1:T(8,128)S(1)}, f32[1024,1,128]{0,2,1:T(8,128)S(1)}, u32[]{:S(2)}, u32[]{:S(2)}) collective-permute-start(f32[1024,1,128]{0,2,1:T(8,128)S(1)} %get-tuple-element.9), channel_id=1, source_target_pairs={{0,4},{1,5},{2,6},{3,7},{8,12},{9,13},{10,14},{11,15},{16,20},{17,... | collective-permute-start | bytes 1572872 | tf_op jit(solution)/shard_map/ppermute | solution.py:16
  189.7 14.1 %collective-permute-start.9 = (f32[1024,1,128]{0,2,1:T(8,128)S(1)}, f32[1024,1,128]{0,2,1:T(8,128)S(1)}, u32[]{:S(2)}, u32[]{:S(2)}) collective-permute-start(f32[1024,1,128]{0,2,1:T(8,128)S(1)} %get-tuple-element.10), channel_id=1, source_target_pairs={{4,0},{5,1},{6,2},{7,3},{12,8},{13,9},{14,10},{15,11},{20,16},{21,... | collective-permute-start | bytes 1572872 | tf_op jit(solution)/shard_map/ppermute | solution.py:17
  203.9 7.0 %collective-permute-start.10 = (f32[1024,10,1]{0,2,1:T(1,128)S(1)}, f32[1024,10,1]{0,2,1:T(1,128)S(1)}, u32[]{:S(2)}, u32[]{:S(2)}) collective-permute-start(f32[1024,10,1]{0,2,1:T(1,128)S(1)} %get-tuple-element.5), channel_id=1, source_target_pairs={{0,1},{1,2},{2,3},{4,5},{5,6},{6,7},{8,9},{9,10},{10,11},{12,13},{... | collective-permute-start | bytes 122888 | tf_op jit(solution)/shard_map/ppermute | solution.py:16
  209.0 5.3 %collective-permute-start.11 = (f32[1024,10,1]{0,2,1:T(1,128)S(1)}, f32[1024,10,1]{0,2,1:T(1,128)S(1)}, u32[]{:S(2)}, u32[]{:S(2)}) collective-permute-start(f32[1024,10,1]{0,2,1:T(1,128)S(1)} %get-tuple-element.6), channel_id=1, source_target_pairs={{1,0},{2,1},{3,2},{5,4},{6,5},{7,6},{9,8},{10,9},{11,10},{13,12},{... | collective-permute-start | bytes 122888 | tf_op jit(solution)/shard_map/ppermute | solution.py:17
Sparse Core Ops, SparseCore 0:
  8.9 45.2 all-gather.1
  97.1 84.7 all-reduce.1
  229.5 39.9 reduce-scatter.1
where the time goes:
time: 285 us; the launch traced here: 281 us
  waiting for transfers between devices  188 us (66%)
  starting transfers between devices  33.7 us (12%)
  matrix products  21.3 us (7%)
  other arithmetic  20.1 us (7%)
  between operations  13.4 us (5%)
  local copies, waits for them, and re-layouts  4.51 us (2%)
    psum x1, waiting for transfers between devices, body(): lax.psum(partial_sum.astype(jnp.bfloat16), 'quad').astype(jnp.float32)  84.7 us
    all_gather x1, waiting for transfers between devices, body(): lax.all_gather(modes_now.reshape(k_local, -1), 'quad', axis=0, tiled=True)  40.2 us
    reduce_scatter x1, waiting for transfers between devices, body(): lax.psum_scatter(lax.dot_general(basis_rows, weighted, (((0,), (0,)), (()...  40.1 us
    ppermute x6, starting transfers between devices, with_halo(): before = lax.ppermute(last, axis, up)  23.8 us
    convert_element_type x2, other arithmetic, drive_with(): (weights[:, None, None] * total).astype(jnp.bfloat16)  16.4 us
    ppermute x6, waiting for transfers between devices, with_halo(): before = lax.ppermute(last, axis, up)  11.7 us
    ppermute x6, waiting for transfers between devices, with_halo(): after = lax.ppermute(leading, axis, down)  11.1 us
    ppermute x6, starting transfers between devices, with_halo(): after = lax.ppermute(leading, axis, down)  9.64 us
  transfers between devices with their start and end apart: 15, of which 8 were waited for; matrix products, arithmetic and copies ran while one was open for 4% of the time, Pallas kernels for 0%

commit v1 on v0

--- a/solution.py
+++ b/solution.py
@@ -1,9 +1,437 @@
+import functools
+
 import jax
 import jax.numpy as jnp
 from jax import lax
+from jax.experimental import pallas as pl
+from jax.experimental.pallas import tpu as pltpu
 from jax.sharding import PartitionSpec as P
 
 time_step = 0.04
+LANES = 128
+GROUP = 16
+NODE_PARTS = (0, 0, 1, 1, 0, 2)
+LOG_PARTS = (0, 1, 0, 1, 2, 0)
+MESH = pl.DeviceIdType.MESH
+
+
+def split_parts(values, pattern):
+    parts, rest = [], values
+    for _ in range(3):
+        part = rest.astype(jnp.bfloat16)
+        parts.append(part.astype(jnp.float32))
+        rest = rest - parts[-1]
+    group = lax.broadcasted_iota(jnp.int32, values.shape, 1) // GROUP
+    chosen = jnp.zeros_like(values)
+    for index, which in enumerate(pattern):
+        chosen = jnp.where(group == index, parts[which], chosen)
+    return chosen.astype(jnp.bfloat16)
+
+
+def spread(columns):
+    padded = jnp.pad(columns, ((0, 0), (0, GROUP - columns.shape[1])))
+    copies = len(NODE_PARTS)
+    return jnp.pad(jnp.tile(padded, (1, copies)), ((0, 0), (0, LANES - copies * GROUP)))
+
+
+def dot_nt(a, b):
+    return lax.dot_general(a, b, (((1,), (1,)), ((), ())), preferred_element_type=jnp.float32)
+
+
+def dot_nn(a, b):
+    return jnp.dot(a, b, preferred_element_type=jnp.float32)
+
+
+def picard_kernel(
+    dims, modes_ref, basis_ref, aux_ref, logs_ref, out_ref,
+    basis, first, second, halo_in, halo_out, field, coeff, weighted, outgoing, landed,
+    local_sem, b_send, b_recv, m_send, m_recv, h_send, h_recv, o_send, o_recv,
+):
+    n, ny, nx, kl, ql, terms, rows, cols, qb = dims
+    modes, cells, rim = n * kl, rows * cols, 2 * rows
+    quad_pts, piece = n * ql, ql // (ny * nx)
+    z, gy, gx = lax.axis_index("quad"), lax.axis_index("gy"), lax.axis_index("gx")
+    even = lax.rem(gx, 2) == 0
+    other_gy = 1 - gy
+    other_core = gx + 1 - 2 * lax.rem(gx, 2)
+    other_x = lax.rem(gx + 2, 4)
+    to_x, to_y, to_core = (z, gy, other_x), (z, other_gy, gx), (z, gy, other_core)
+    own = pl.ds(rim, cells)
+
+    def block_of(rank):
+        return jnp.where(even, rank, n - 1 - rank)
+
+    def remote(src, dst, send, recv, target):
+        return pltpu.make_async_remote_copy(
+            src_ref=src, dst_ref=dst, send_sem=send, recv_sem=recv,
+            device_id=target, device_id_type=MESH,
+        )
+
+    barrier = pltpu.get_barrier_semaphore()
+    for step in range(1, n):
+        pl.semaphore_signal(barrier, inc=1, device_id=(lax.rem(z + step, n), gy, gx), device_id_type=MESH)
+    for step in range(1, nx):
+        pl.semaphore_signal(barrier, inc=1, device_id=(z, gy, lax.rem(gx + step, nx)), device_id_type=MESH)
+    pl.semaphore_signal(barrier, inc=1, device_id=to_y, device_id_type=MESH)
+    pl.semaphore_wait(barrier, n + nx - 1)
+
+    def modes_copy(rank):
+        rows_of = pl.multiple_of(block_of(rank) * cells, cells)
+        return modes_ref.at[pl.ds(rows_of, cells), :]
+
+    def modes_slot(rank):
+        return first.at[own, pl.ds(pl.multiple_of(rank * kl, kl), kl)]
+
+    def peer(step):
+        return lax.rem(z + step, n)
+
+    load_basis = pltpu.make_async_copy(
+        basis_ref, basis.at[pl.ds(pl.multiple_of(z * ql, ql), ql), pl.ds(0, modes)], local_sem.at[0]
+    )
+    load_basis.start()
+    for step in range(1, n):
+        remote(modes_copy(peer(step)), modes_slot(z), m_send.at[step], m_recv.at[step], (peer(step), gy, gx)).start()
+    load_modes = pltpu.make_async_copy(modes_copy(z), modes_slot(z), local_sem.at[1])
+    load_modes.start()
+    basis[pl.ds(pl.multiple_of(z * ql, ql), ql), modes : modes + LANES] = split_parts(aux_ref[...], NODE_PARTS)
+    load_basis.wait()
+
+    def rows_at(shard, y, x, part=None):
+        start = shard * ql + (y * nx + x) * piece
+        if part is None:
+            return basis.at[pl.ds(pl.multiple_of(start, piece), piece), :]
+        half = piece // 2
+        return basis.at[pl.ds(pl.multiple_of(start + part * half, half), half), :]
+
+    Z, X, Y, DA, DB, S0, SX, SY, SA, SB, ZB = range(11)
+
+    def push(ref, shard, kind, target, send_kind=None):
+        send_kind = kind if send_kind is None else send_kind
+        return remote(ref, ref, b_send.at[shard, send_kind], b_recv.at[shard, kind], target)
+
+    def arrived(ref, shard, kind):
+        push(ref, shard, kind, to_core).wait_recv()
+
+    def up(shard):
+        return push(rows_at(shard, gy, gx), shard, Z, (jnp.minimum(z + 1, n - 1), gy, gx))
+
+    def down(shard):
+        return push(rows_at(shard, gy, gx), shard, Z, (jnp.maximum(z - 1, 0), gy, gx), ZB)
+
+    @pl.when(z < n - 1)
+    def _():
+        up(z).start()
+
+    @pl.when(z > 0)
+    def _():
+        down(z).start()
+
+    def plane(shard):
+        mine = rows_at(shard, gy, gx)
+        return [push(mine, shard, X, to_x), push(mine, shard, Y, to_y), push(mine, shard, S0, to_core)]
+
+    def relay(shard):
+        by_x, by_y = rows_at(shard, gy, other_x), rows_at(shard, other_gy, gx)
+        return (
+            [push(rows_at(shard, gy, other_x, 0), shard, DA, to_y), push(by_x, shard, SX, to_core)],
+            [push(rows_at(shard, other_gy, gx, 1), shard, DB, to_x), push(by_y, shard, SY, to_core)],
+        )
+
+    def across(shard):
+        return [
+            push(rows_at(shard, other_gy, other_x, 0), shard, SA, to_core),
+            push(rows_at(shard, other_gy, other_x, 1), shard, SB, to_core),
+        ]
+
+    def stage_z(shard):
+        arrived(rows_at(shard, gy, gx), shard, Z)
+        for copy in plane(shard):
+            copy.start()
+
+        @pl.when((shard < z) & (z < n - 1))
+        def _():
+            up(shard).start()
+
+        @pl.when((shard > z) & (z > 0))
+        def _():
+            down(shard).start()
+
+    def stage_xy(shard):
+        after_x, after_y = relay(shard)
+        arrived(rows_at(shard, gy, other_x), shard, X)
+        for copy in after_x:
+            copy.start()
+        arrived(rows_at(shard, other_gy, gx), shard, Y)
+        for copy in after_y:
+            copy.start()
+
+    def stage_d(shard):
+        one, two = across(shard)
+        arrived(rows_at(shard, other_gy, other_x, 0), shard, DA)
+        one.start()
+        arrived(rows_at(shard, other_gy, other_x, 1), shard, DB)
+        two.start()
+
+    def stage_s(shard):
+        arrived(rows_at(shard, gy, other_core), shard, S0)
+        core_x = lax.rem(other_core + 2, 4)
+        arrived(rows_at(shard, gy, core_x), shard, SX)
+        arrived(rows_at(shard, other_gy, other_core), shard, SY)
+        arrived(rows_at(shard, other_gy, core_x, 0), shard, SA)
+        arrived(rows_at(shard, other_gy, core_x, 1), shard, SB)
+
+    def drain(shard):
+        for copy in plane(shard) + relay(shard)[0] + relay(shard)[1] + across(shard):
+            copy.wait_send()
+
+        @pl.when((shard < z) & (z < n - 1))
+        def _():
+            up(shard).wait_send()
+
+        @pl.when((shard > z) & (z > 0))
+        def _():
+            down(shard).wait_send()
+
+    block = block_of(z)
+    ahead = jnp.where(even, 1, -1)
+    in_right, in_left = block < n - 1, block > 0
+    has_right, has_left = in_right | (gx < nx - 1), in_left | (gx > 0)
+    right_z, left_z = jnp.where(in_right, z + ahead, z), jnp.where(in_left, z - ahead, z)
+    right_x = jnp.where(in_right, gx, jnp.minimum(gx + 1, nx - 1))
+    left_x = jnp.where(in_left, gx, jnp.maximum(gx - 1, 0))
+
+    def halo(turn, grid):
+        width = grid.shape[1]
+        span = pl.ds(0, width)
+        hr, hs = h_recv, h_send
+        lead, tail = grid.at[pl.ds(rim, rim), span], grid.at[pl.ds(cells, rim), span]
+        before, after = grid.at[pl.ds(0, rim), span], grid.at[pl.ds(rim + cells, rim), span]
+        top, bottom = halo_in.at[turn, pl.ds(0, cols), span], halo_in.at[turn, pl.ds(cols, cols), span]
+        mine_last = halo_out.at[turn, pl.ds(0, cols), span]
+        mine_lead = halo_out.at[turn, pl.ds(cols, cols), span]
+        row = lax.broadcasted_iota(jnp.int32, (2 * cols, cells), 0)
+        cell = lax.broadcasted_iota(jnp.int32, (2 * cols, cells), 1)
+        wanted = jnp.where(row < cols, row * rows + rows - 1, (row - cols) * rows)
+        pick = (wanted == cell).astype(jnp.float32).astype(jnp.bfloat16)
+
+        steps = (
+            (has_right, remote(tail, before, hs.at[turn, 0], hr.at[turn, 0], (right_z, gy, right_x)), has_left, before),
+            (has_left, remote(lead, after, hs.at[turn, 1], hr.at[turn, 1], (left_z, gy, left_x)), has_right, after),
+            (gy < ny - 1, remote(mine_last, top, hs.at[turn, 2], hr.at[turn, 2], to_y), gy > 0, top),
+            (gy > 0, remote(mine_lead, bottom, hs.at[turn, 3], hr.at[turn, 3], to_y), gy < ny - 1, bottom),
+        )
+
+        def start():
+            halo_out[turn, :, 0:width] = dot_nn(pick, grid[rim : rim + cells, :]).astype(jnp.bfloat16)
+            for sends, copy, gets, slot in steps:
+
+                @pl.when(sends)
+                def _():
+                    copy.start()
+
+                @pl.when(jnp.logical_not(gets))
+                def _():
+                    slot[...] = jnp.zeros(slot.shape, jnp.bfloat16)
+
+        def finish():
+            for sends, copy, gets, slot in steps:
+
+                @pl.when(gets)
+                def _():
+                    copy.wait_recv()
+
+            cell_t = lax.broadcasted_iota(jnp.int32, (cells, 2 * cols), 0)
+            row_t = lax.broadcasted_iota(jnp.int32, (cells, 2 * cols), 1)
+            goal = jnp.where(row_t < cols, row_t * rows, (row_t - cols) * rows + rows - 1)
+            place = (goal == cell_t).astype(jnp.float32).astype(jnp.bfloat16)
+            grid[2 * rim + cells : 2 * rim + 2 * cells, :] = dot_nn(
+                place, halo_in[turn, :, 0:width]
+            ).astype(jnp.bfloat16)
+
+        def drained():
+            for sends, copy, gets, slot in steps:
+
+                @pl.when(sends)
+                def _():
+                    copy.wait_send()
+
+        return start, finish, drained
+
+    lane = lax.broadcasted_iota(jnp.int32, (GROUP, LANES), 1)
+    line = lax.broadcasted_iota(jnp.int32, (GROUP, LANES), 0)
+    group = lane // GROUP
+    whole = (group == 0) | (group == 2) | (group == 5)
+    wants = (lane - group * GROUP) == terms + line
+    select = jnp.where(whole & wants & (line < 2), 1.0, 0.0).astype(jnp.bfloat16)
+    lanes = min(256, qb)
+    slab = 2 * rows
+
+    def drive(shard, grid):
+        def step(i, _):
+            start = pl.multiple_of(shard * ql + i * qb, qb)
+            ext = basis[pl.ds(start, qb), modes : modes + LANES]
+            field[...] = dot_nt(grid[:, 0:modes], basis[pl.ds(start, qb), 0:modes])
+            coeff[...] = jnp.exp(dot_nt(first[:, modes : modes + LANES], ext))
+            scalars = dot_nt(select, ext)
+            y_at = lax.broadcasted_iota(jnp.int32, (2, rows, lanes), 1)
+            for h in range(qb // lanes):
+                part = slice(h * lanes, (h + 1) * lanes)
+                weight, rate = scalars[0:1, part], scalars[1:2, part]
+                for c in range(cells // slab):
+
+                    def at(ref, offset):
+                        return ref[offset + c * slab : offset + (c + 1) * slab, part]
+
+                    mid, cm = at(field, rim), at(coeff, rim)
+                    total = (cm + at(coeff, rim - rows)) * (at(field, rim - rows) - mid)
+                    total += (cm + at(coeff, rim + rows)) * (at(field, rim + rows) - mid)
+                    mid3, cm3 = mid.reshape(2, rows, lanes), cm.reshape(2, rows, lanes)
+                    fh = at(field, 2 * rim + cells).reshape(2, rows, lanes)
+                    ch = at(coeff, 2 * rim + cells).reshape(2, rows, lanes)
+                    for shift, edge in ((1, 0), (rows - 1, rows - 1)):
+                        fn = jnp.where(y_at == edge, fh, pltpu.roll(mid3, shift, 1))
+                        cn = jnp.where(y_at == edge, ch, pltpu.roll(cm3, shift, 1))
+                        total += ((cm3 + cn) * (fn - mid3)).reshape(slab, lanes)
+                    total += rate * (mid - mid * mid * mid)
+                    weighted[c * slab : (c + 1) * slab, pl.ds(start + h * lanes, lanes)] = (
+                        weight * total
+                    ).astype(jnp.bfloat16)
+            return 0
+
+        lax.fori_loop(0, ql // qb, step, 0)
+
+    first[own, modes : modes + LANES] = split_parts(
+        logs_ref[pl.ds(pl.multiple_of(block * cells, cells), cells), :], LOG_PARTS
+    )
+    load_modes.wait()
+    for step in range(1, n):
+        source = lax.rem(z - step + n, n)
+        remote(modes_slot(source), modes_slot(source), m_send.at[step], m_recv.at[step], to_y).wait_recv()
+    halo_a = halo(0, first)
+    halo_a[0]()
+
+    def nth(j):
+        shard = jnp.int32(0)
+        for rank in range(n):
+            order = sorted((s for s in range(n) if s != rank), key=lambda s: (abs(s - rank), s))
+            shard = shard + jnp.where(z == rank, order[j], 0)
+        return shard
+
+    shards = [nth(j) for j in range(n - 1)]
+    stages = (stage_z, stage_xy, stage_d)
+    stage_z(shards[0])
+    halo_a[1]()
+    drive(z, first)
+    for turn in range(1, n + 1):
+        for depth, stage in reversed(list(enumerate(stages))):
+            j = turn - depth
+            if 0 <= j < n - 1 and (j, depth) != (0, 0):
+                stage(shards[j])
+        j = turn - 2
+        if 0 <= j < n - 1:
+            stage_s(shards[j])
+            drive(shards[j], first)
+
+    def project(rank):
+        span = pl.ds(pl.multiple_of(rank * kl, kl), kl)
+        return span, dot_nn(weighted[...], basis[:, span])
+
+    def update(rank, _):
+        span, got = project(rank)
+        now = first[own, span].astype(jnp.float32)
+        second[own, span] = (now + time_step * got).astype(jnp.bfloat16)
+        return 0
+
+    lax.fori_loop(0, n, update, 0)
+
+    halo_b = halo(1, second)
+    halo_b[0]()
+    halo_b[1]()
+    lax.fori_loop(0, n, lambda shard, _: (drive(shard, second), 0)[1], 0)
+
+    def landing(owner_block):
+        return landed.at[pl.ds(pl.multiple_of(owner_block * cells, cells), cells), :]
+
+    def deliver(step):
+        return remote(
+            outgoing.at[step], landing(block), o_send.at[step], o_recv.at[step], (peer(step), gy, gx)
+        )
+
+    for step in range(1, n):
+        outgoing[step] = project(peer(step))[1].astype(jnp.bfloat16)
+        deliver(step).start()
+    landed[pl.ds(pl.multiple_of(block * cells, cells), cells), :] = project(z)[1].astype(jnp.bfloat16)
+    for step in range(1, n):
+        source = landing(block_of(lax.rem(z - step + n, n)))
+        remote(source, source, o_send.at[step], o_recv.at[step], to_y).wait_recv()
+    out_ref[...] = landed[...]
+
+    for step in range(1, n):
+        deliver(step).wait_send()
+        remote(modes_copy(peer(step)), modes_slot(z), m_send.at[step], m_recv.at[step], (peer(step), gy, gx)).wait_send()
+    halo_a[2]()
+    halo_b[2]()
+
+    @pl.when(z < n - 1)
+    def _():
+        up(z).wait_send()
+
+    @pl.when(z > 0)
+    def _():
+        down(z).wait_send()
+
+    for shard in shards:
+        drain(shard)
+
+
+def fast_body(n, ny, nx, modes_now, basis_rows, quad_weights, germ_nodes, log_fields, reaction_rates):
+    kl, rows, width = modes_now.shape
+    ql, modes = basis_rows.shape
+    terms = germ_nodes.shape[1]
+    cols = width // n
+    cells, tile, rim, quad_pts = rows * cols, rows * width, 2 * rows, n * ql
+    qb = min(512, ql)
+    ext = modes + LANES
+    dims = (n, ny, nx, kl, ql, terms, rows, cols, qb)
+    modes_t = modes_now.transpose(2, 1, 0).reshape(tile, kl)
+    aux = spread(jnp.concatenate([germ_nodes, quad_weights[:, None], reaction_rates[:, None]], axis=1))
+    logs = spread(log_fields.transpose(2, 1, 0).reshape(tile, terms))
+    any_spec, vmem = pl.BlockSpec(memory_space=pl.ANY), pl.BlockSpec(memory_space=pltpu.VMEM)
+    grid_rows = 2 * rim + 2 * cells
+    bf16, f32 = jnp.bfloat16, jnp.float32
+    dma = pltpu.SemaphoreType.DMA
+    delta_t = pl.pallas_call(
+        functools.partial(picard_kernel, dims),
+        out_shape=jax.ShapeDtypeStruct((tile, kl), bf16),
+        in_specs=[any_spec, any_spec, vmem, vmem],
+        out_specs=vmem,
+        scratch_shapes=[
+            pltpu.VMEM((quad_pts, ext), bf16),
+            pltpu.VMEM((grid_rows, ext), bf16),
+            pltpu.VMEM((grid_rows, modes), bf16),
+            pltpu.VMEM((2, 2 * cols, ext), bf16),
+            pltpu.VMEM((2, 2 * cols, ext), bf16),
+            pltpu.VMEM((grid_rows, qb), f32),
+            pltpu.VMEM((grid_rows, qb), f32),
+            pltpu.VMEM((cells, quad_pts), bf16),
+            pltpu.VMEM((n, cells, kl), bf16),
+            pltpu.VMEM((tile, kl), bf16),
+            dma((2,)),
+            dma((n, 11)),
+            dma((n, 11)),
+            dma((n,)),
+            dma((n,)),
+            dma((2, 4)),
+            dma((2, 4)),
+            dma((n,)),
+            dma((n,)),
+        ],
+        compiler_params=pltpu.CompilerParams(
+            collective_id=0, has_side_effects=True, vmem_limit_bytes=48 * 1024 * 1024
+        ),
+    )(modes_t, basis_rows, aux, logs)
+    delta = delta_t.reshape(width, rows, kl).transpose(2, 1, 0)
+    return modes_now.astype(f32) + time_step * delta.astype(f32)
 
 
 def with_halo(array, sides, width):
@@ -88,6 +516,9 @@
 
 
 def solution(mesh):
+    n, ny, nx = (mesh.shape[name] for name in ("quad", "gy", "gx"))
+    planar = (ny, nx) == (2, 4) and n > 1
+    run = functools.partial(fast_body, n, ny, nx) if planar else body
     in_specs = (
         P("quad", "gy", "gx"),
         P("quad", None),
@@ -97,4 +528,4 @@
         P("quad"),
     )
     out_specs = P("quad", "gy", "gx")
-    return jax.shard_map(body, mesh=mesh, in_specs=in_specs, out_specs=out_specs, check_vma=False)
+    return jax.shard_map(run, mesh=mesh, in_specs=in_specs, out_specs=out_specs, check_vma=False)

time: 285 us -> 103 us (0.36); the launches traced: 281 us -> 102 us
  waiting for transfers between devices: 188 us -> 0 us
  Pallas kernels: 0 us -> 94.8 us
  starting transfers between devices: 33.7 us -> 0 us
  matrix products: 21.3 us -> 0 us
  other arithmetic: 20.1 us -> 1.96 us
  between operations: 13.4 us -> 0.13 us
    pallas_call x0 -> x1, Pallas kernels: none -> 94.8 us  [fast_body(): pl.pallas_call(functools.partial(picard_kernel, dims), out_shape=jax.Shap...]
    psum x1 -> x0, waiting for transfers between devices: 84.7 us -> none  [body(): lax.psum(partial_sum.astype(jnp.bfloat16), 'quad').astype(jnp.float32)]
    all_gather x1 -> x0, waiting for transfers between devices: 40.2 us -> none  [body(): lax.all_gather(modes_now.reshape(k_local, -1), 'quad', axis=0, tiled=True)]
    reduce_scatter x1 -> x0, waiting for transfers between devices: 40.1 us -> none  [body(): lax.psum_scatter(lax.dot_general(basis_rows, weighted, (((0,), (0,)), (()...]
    ppermute x12 -> x0, starting transfers between devices: 33.4 us -> none  [the longest x6 23.8 us: with_halo(): before = lax.ppermute(last, axis, up)]
    ppermute x12 -> x0, waiting for transfers between devices: 22.8 us -> none  [the longest x6 11.7 us: with_halo(): before = lax.ppermute(last, axis, up)]
    dot_general x5 -> x0, matrix products: 21.3 us -> none  [the longest x1 5.22 us: body(): jnp.einsum('qj,jyx->qyx', germ_nodes, log_ext, precision=lax.Precision.HI...]
    convert_element_type x2 -> x0, other arithmetic: 16.4 us -> none  [drive_with(): (weights[:, None, None] * total).astype(jnp.bfloat16)]
  transfers between devices with their start and end apart: 15 -> 0, of which waited for: 8 -> 0; matrix products, arithmetic and copies ran while one was open for 4% -> 0% of each run, Pallas kernels for 0% -> 0%
where the time goes in v1:
time: 103 us; the launch traced here: 102 us
  Pallas kernels  94.8 us (92%)
  local copies, waits for them, and re-layouts  5.36 us (5%)
  other arithmetic  1.96 us (2%)
    pallas_call x1, Pallas kernels, fast_body(): pl.pallas_call(functools.partial(picard_kernel, dims), out_shape=jax.Shap...  94.8 us

profile of v1, /device:TPU:9, one launch (start us, length us, event | category | flops | bytes accessed | tf_op | source)
XLA Modules:
  0.0 102.3 jit_solution(1034489583315903765)
XLA Ops:
  0.0 0.0 copy-start.3
  0.0 0.8 select_maximum_fusion
  0.9 0.2 copy.11
  1.1 0.0 copy-done.3
  1.1 0.2 copy.12
  1.3 0.0 copy-start
  1.3 0.3 reshape.19
  1.6 0.2 copy.13
  1.8 0.8 pad.18.logs_ref
  2.7 1.6 %copy.10 = bf16[128,8,256]{2,1,0:T(8,128)(2,1)S(1)} copy(bf16[128,8,256]{0,1,2:T(8,128)(2,1)} %bitcast.14) | data formatting | bytes 1048576 | tf_op jit(solution)/shard_map/transpose | solution.py:396
  4.3 0.0 copy-done
  4.3 0.0 copy-start.1
  4.3 1.0 %copy-done.1 = f32[1024,128]{1,0:T(8,128)S(1)} copy-done((f32[1024,128]{1,0:T(8,128)S(1)}, f32[1024,128]{1,0:T(8,128)}, u32[]{:S(2)}) %copy-start.1) | copy-done | bytes 524312
  5.3 94.8 %shard_map.64 = bf16[1024,256]{1,0:T(8,128)(2,1)S(1)} custom-call(bf16[1024,256]{1,0:T(8,128)(2,1)S(1)} %bitcast.13, bf16[1024,1024]{1,0:T(8,128)(2,1)S(1)} %copy-done, f32[1024,128]{1,0:T(8,128)S(1)} %pad.16.aux_ref, f32[1024,128]{1,0:T(8,128)S(1)} %copy-done.1), custom_call_target="tpu_custom_call" | custom-call | tf_op jit(solution)/shard_map/pallas_call | solution.py:403
  100.2 0.0 copy-start.2
  100.2 0.1 multiply_bitcast_fusion
  100.3 0.6 copy.14
  100.8 0.4 copy-done.2
  101.2 1.1 %bitcast_add_fusion = f32[256,8,128]{2,1,0:T(8,128)} fusion(f32[128,8,256]{0,1,2:T(8,128)S(1)} %copy.14, bf16[256,8,128]{2,1,0:T(8,128)(2,1)S(1)} %copy-done.2), kind=kLoop, calls=%fused_computation | loop fusion | flops 524288 | bytes 2621440 | tf_op jit(solution)/shard_map/add | solution.py:434
  (4 shorter events, 0.1 us)
Async XLA Ops:
  0.0 1.1 %copy-start.3 = (f32[8,8,128]{2,1,0:T(8,128)S(1)}, f32[8,8,128]{2,1,0:T(8,128)}, u32[]{:S(2)}) copy-start(f32[8,8,128]{2,1,0:T(8,128)} %param.10) | copy-start | bytes 98308
  1.3 3.0 %copy-start = (bf16[1024,1024]{1,0:T(8,128)(2,1)S(1)}, bf16[1024,1024]{1,0:T(8,128)(2,1)}, u32[]{:S(2)}) copy-start(bf16[1024,1024]{1,0:T(8,128)(2,1)} %basis_ref.1) | copy-start | bytes 6291460
  4.3 1.0 %copy-start.1 = (f32[1024,128]{1,0:T(8,128)S(1)}, f32[1024,128]{1,0:T(8,128)}, u32[]{:S(2)}) copy-start(f32[1024,128]{1,0:T(8,128)} %pad.18.logs_ref) | copy-start | bytes 1572868
  100.2 1.0 %copy-start.2 = (bf16[256,8,128]{2,1,0:T(8,128)(2,1)S(1)}, bf16[256,8,128]{2,1,0:T(8,128)(2,1)}, u32[]{:S(2)}) copy-start(bf16[256,8,128]{2,1,0:T(8,128)(2,1)} %param.6) | copy-start | bytes 1572868

commit v2 on v1

--- a/solution.py
+++ b/solution.py
@@ -44,7 +44,7 @@
 
 def picard_kernel(
     dims, modes_ref, basis_ref, aux_ref, logs_ref, out_ref,
-    basis, first, second, halo_in, halo_out, field, coeff, weighted, outgoing, landed,
+    basis, first, second, halo_out, field_a, field_b, coeff, faces, weighted, outgoing, landed,
     local_sem, b_send, b_recv, m_send, m_recv, h_send, h_recv, o_send, o_recv,
 ):
     n, ny, nx, kl, ql, terms, rows, cols, qb = dims
@@ -56,7 +56,7 @@
     other_core = gx + 1 - 2 * lax.rem(gx, 2)
     other_x = lax.rem(gx + 2, 4)
     to_x, to_y, to_core = (z, gy, other_x), (z, other_gy, gx), (z, gy, other_core)
-    own = pl.ds(rim, cells)
+    own, edge = pl.ds(rim, cells), 2 * rim + cells
 
     def block_of(rank):
         return jnp.where(even, rank, n - 1 - rank)
@@ -206,7 +206,7 @@
         hr, hs = h_recv, h_send
         lead, tail = grid.at[pl.ds(rim, rim), span], grid.at[pl.ds(cells, rim), span]
         before, after = grid.at[pl.ds(0, rim), span], grid.at[pl.ds(rim + cells, rim), span]
-        top, bottom = halo_in.at[turn, pl.ds(0, cols), span], halo_in.at[turn, pl.ds(cols, cols), span]
+        top, bottom = grid.at[pl.ds(edge, cols), span], grid.at[pl.ds(edge + cols, cols), span]
         mine_last = halo_out.at[turn, pl.ds(0, cols), span]
         mine_lead = halo_out.at[turn, pl.ds(cols, cols), span]
         row = lax.broadcasted_iota(jnp.int32, (2 * cols, cells), 0)
@@ -239,14 +239,6 @@
                 @pl.when(gets)
                 def _():
                     copy.wait_recv()
-
-            cell_t = lax.broadcasted_iota(jnp.int32, (cells, 2 * cols), 0)
-            row_t = lax.broadcasted_iota(jnp.int32, (cells, 2 * cols), 1)
-            goal = jnp.where(row_t < cols, row_t * rows, (row_t - cols) * rows + rows - 1)
-            place = (goal == cell_t).astype(jnp.float32).astype(jnp.bfloat16)
-            grid[2 * rim + cells : 2 * rim + 2 * cells, :] = dot_nn(
-                place, halo_in[turn, :, 0:width]
-            ).astype(jnp.bfloat16)
 
         def drained():
             for sends, copy, gets, slot in steps:
@@ -266,39 +258,79 @@
     lanes = min(256, qb)
     slab = 2 * rows
 
-    def drive(shard, grid):
-        def step(i, _):
-            start = pl.multiple_of(shard * ql + i * qb, qb)
-            ext = basis[pl.ds(start, qb), modes : modes + LANES]
-            field[...] = dot_nt(grid[:, 0:modes], basis[pl.ds(start, qb), 0:modes])
+    def start_of(block_index):
+        return pl.multiple_of(block_index * qb, qb)
+
+    def multiply(field, block_index, grid):
+        field[...] = dot_nt(grid[:, 0:modes], basis[pl.ds(start_of(block_index), qb), 0:modes])
+
+    def drive(field, block_index, fresh):
+        start = start_of(block_index)
+        ext = basis[pl.ds(start, qb), modes : modes + LANES]
+        scalars = dot_nt(select, ext)
+        if fresh:
             coeff[...] = jnp.exp(dot_nt(first[:, modes : modes + LANES], ext))
-            scalars = dot_nt(select, ext)
-            y_at = lax.broadcasted_iota(jnp.int32, (2, rows, lanes), 1)
-            for h in range(qb // lanes):
-                part = slice(h * lanes, (h + 1) * lanes)
-                weight, rate = scalars[0:1, part], scalars[1:2, part]
-                for c in range(cells // slab):
-
-                    def at(ref, offset):
-                        return ref[offset + c * slab : offset + (c + 1) * slab, part]
-
-                    mid, cm = at(field, rim), at(coeff, rim)
-                    total = (cm + at(coeff, rim - rows)) * (at(field, rim - rows) - mid)
-                    total += (cm + at(coeff, rim + rows)) * (at(field, rim + rows) - mid)
-                    mid3, cm3 = mid.reshape(2, rows, lanes), cm.reshape(2, rows, lanes)
-                    fh = at(field, 2 * rim + cells).reshape(2, rows, lanes)
-                    ch = at(coeff, 2 * rim + cells).reshape(2, rows, lanes)
-                    for shift, edge in ((1, 0), (rows - 1, rows - 1)):
-                        fn = jnp.where(y_at == edge, fh, pltpu.roll(mid3, shift, 1))
-                        cn = jnp.where(y_at == edge, ch, pltpu.roll(cm3, shift, 1))
-                        total += ((cm3 + cn) * (fn - mid3)).reshape(slab, lanes)
-                    total += rate * (mid - mid * mid * mid)
-                    weighted[c * slab : (c + 1) * slab, pl.ds(start + h * lanes, lanes)] = (
-                        weight * total
-                    ).astype(jnp.bfloat16)
+        y_at = lax.broadcasted_iota(jnp.int32, (rows, lanes), 0)
+        for h in range(qb // lanes):
+            part = slice(h * lanes, (h + 1) * lanes)
+            here = pl.ds(start + h * lanes, lanes)
+            weight, rate = scalars[0:1, part], scalars[1:2, part]
+
+            def sides(ref, column):
+                low = rim + column * rows
+                mid = ref[low : low + rows, part]
+                above = ref[edge + column : edge + column + 1, part]
+                below = ref[edge + cols + column : edge + cols + column + 1, part]
+                return mid, (
+                    ref[low - rows : low, part],
+                    ref[low + rows : low + 2 * rows, part],
+                    jnp.where(y_at == 0, above, pltpu.roll(mid, 1, 0)),
+                    jnp.where(y_at == rows - 1, below, pltpu.roll(mid, rows - 1, 0)),
+                )
+
+            for c in range(cols // 2):
+                results = []
+                for column in (2 * c, 2 * c + 1):
+                    at = slice(column * rows, (column + 1) * rows)
+                    mid, around = sides(field, column)
+                    if fresh:
+                        cm, others = sides(coeff, column)
+                        sums = [cm + other for other in others]
+                        for side, value in enumerate(sums):
+                            faces[side, at, here] = value
+                    else:
+                        sums = [faces[side, at, here] for side in range(4)]
+                    total = rate * (mid - mid * mid * mid)
+                    for value, other in zip(sums, around):
+                        total += value * (other - mid)
+                    results.append(weight * total)
+                weighted[c * slab : (c + 1) * slab, here] = jnp.concatenate(results, axis=0).astype(
+                    jnp.bfloat16
+                )
+
+    per_shard = ql // qb
+    fields = (field_a, field_b)
+
+    def drive_shard(shard):
+        base = shard * per_shard
+        multiply(fields[0], base, first)
+        for i in range(per_shard):
+            if i + 1 < per_shard:
+                multiply(fields[(i + 1) % 2], base + i + 1, first)
+            drive(fields[i % 2], base + i, True)
+
+    def drive_all():
+        count = n * per_shard
+
+        def pair(i, _):
+            multiply(field_b, 2 * i + 1, second)
+            drive(field_a, 2 * i, False)
+            multiply(field_a, jnp.minimum(2 * i + 2, count - 1), second)
+            drive(field_b, 2 * i + 1, False)
             return 0
 
-        lax.fori_loop(0, ql // qb, step, 0)
+        multiply(field_a, 0, second)
+        lax.fori_loop(0, count // 2, pair, 0)
 
     first[own, modes : modes + LANES] = split_parts(
         logs_ref[pl.ds(pl.multiple_of(block * cells, cells), cells), :], LOG_PARTS
@@ -321,7 +353,7 @@
     stages = (stage_z, stage_xy, stage_d)
     stage_z(shards[0])
     halo_a[1]()
-    drive(z, first)
+    drive_shard(z)
     for turn in range(1, n + 1):
         for depth, stage in reversed(list(enumerate(stages))):
             j = turn - depth
@@ -330,7 +362,7 @@
         j = turn - 2
         if 0 <= j < n - 1:
             stage_s(shards[j])
-            drive(shards[j], first)
+            drive_shard(shards[j])
 
     def project(rank):
         span = pl.ds(pl.multiple_of(rank * kl, kl), kl)
@@ -347,7 +379,7 @@
     halo_b = halo(1, second)
     halo_b[0]()
     halo_b[1]()
-    lax.fori_loop(0, n, lambda shard, _: (drive(shard, second), 0)[1], 0)
+    drive_all()
 
     def landing(owner_block):
         return landed.at[pl.ds(pl.multiple_of(owner_block * cells, cells), cells), :]
@@ -397,7 +429,7 @@
     aux = spread(jnp.concatenate([germ_nodes, quad_weights[:, None], reaction_rates[:, None]], axis=1))
     logs = spread(log_fields.transpose(2, 1, 0).reshape(tile, terms))
     any_spec, vmem = pl.BlockSpec(memory_space=pl.ANY), pl.BlockSpec(memory_space=pltpu.VMEM)
-    grid_rows = 2 * rim + 2 * cells
+    grid_rows = 2 * rim + cells + 2 * cols
     bf16, f32 = jnp.bfloat16, jnp.float32
     dma = pltpu.SemaphoreType.DMA
     delta_t = pl.pallas_call(
@@ -410,9 +442,10 @@
             pltpu.VMEM((grid_rows, ext), bf16),
             pltpu.VMEM((grid_rows, modes), bf16),
             pltpu.VMEM((2, 2 * cols, ext), bf16),
-            pltpu.VMEM((2, 2 * cols, ext), bf16),
             pltpu.VMEM((grid_rows, qb), f32),
             pltpu.VMEM((grid_rows, qb), f32),
+            pltpu.VMEM((grid_rows, qb), f32),
+            pltpu.VMEM((4, cells, quad_pts), f32),
             pltpu.VMEM((cells, quad_pts), bf16),
             pltpu.VMEM((n, cells, kl), bf16),
             pltpu.VMEM((tile, kl), bf16),

time: 103 us -> 98.4 us (0.955)
  Pallas kernels: 94.8 us -> 90.7 us
    pallas_call x1, Pallas kernels: 94.8 us -> 90.7 us  [fast_body(): pl.pallas_call(functools.partial(picard_kernel, dims), out_shape=jax.Shap...]
where the time goes in v2:
time: 98.4 us; the launch traced here: 98.1 us
  Pallas kernels  90.7 us (92%)
  local copies, waits for them, and re-layouts  5.36 us (5%)
  other arithmetic  1.96 us (2%)
    pallas_call x1, Pallas kernels, fast_body(): pl.pallas_call(functools.partial(picard_kernel, dims), out_shape=jax.Shap...  90.7 us

profile of v2, /device:TPU:9, one launch (start us, length us, event | category | flops | bytes accessed | tf_op | source)
XLA Modules:
  0.0 98.1 jit_solution(1984291843991302405)
XLA Ops:
  0.0 0.0 copy-start.3
  0.0 0.8 select_maximum_fusion
  0.9 0.2 copy.11
  1.1 0.0 copy-done.3
  1.1 0.2 copy.12
  1.3 0.0 copy-start
  1.3 0.3 reshape.19
  1.6 0.2 copy.13
  1.8 0.8 pad.18.logs_ref
  2.7 1.6 %copy.10 = bf16[128,8,256]{2,1,0:T(8,128)(2,1)S(1)} copy(bf16[128,8,256]{0,1,2:T(8,128)(2,1)} %bitcast.14) | data formatting | bytes 1048576 | tf_op jit(solution)/shard_map/transpose | solution.py:428
  4.3 0.0 copy-done
  4.3 0.0 copy-start.1
  4.3 1.0 %copy-done.1 = f32[1024,128]{1,0:T(8,128)S(1)} copy-done((f32[1024,128]{1,0:T(8,128)S(1)}, f32[1024,128]{1,0:T(8,128)}, u32[]{:S(2)}) %copy-start.1) | copy-done | bytes 524312
  5.3 90.7 %shard_map.64 = bf16[1024,256]{1,0:T(8,128)(2,1)S(1)} custom-call(bf16[1024,256]{1,0:T(8,128)(2,1)S(1)} %bitcast.13, bf16[1024,1024]{1,0:T(8,128)(2,1)S(1)} %copy-done, f32[1024,128]{1,0:T(8,128)S(1)} %pad.16.aux_ref, f32[1024,128]{1,0:T(8,128)S(1)} %copy-done.1), custom_call_target="tpu_custom_call" | custom-call | tf_op jit(solution)/shard_map/pallas_call | solution.py:435
  96.0 0.0 copy-start.2
  96.0 0.1 multiply_bitcast_fusion
  96.1 0.6 copy.14
  96.7 0.4 copy-done.2
  97.0 1.1 %bitcast_add_fusion = f32[256,8,128]{2,1,0:T(8,128)} fusion(f32[128,8,256]{0,1,2:T(8,128)S(1)} %copy.14, bf16[256,8,128]{2,1,0:T(8,128)(2,1)S(1)} %copy-done.2), kind=kLoop, calls=%fused_computation | loop fusion | flops 524288 | bytes 2621440 | tf_op jit(solution)/shard_map/add | solution.py:467
  (4 shorter events, 0.1 us)
Async XLA Ops:
  0.0 1.1 %copy-start.3 = (f32[8,8,128]{2,1,0:T(8,128)S(1)}, f32[8,8,128]{2,1,0:T(8,128)}, u32[]{:S(2)}) copy-start(f32[8,8,128]{2,1,0:T(8,128)} %param.10) | copy-start | bytes 98308
  1.3 3.0 %copy-start = (bf16[1024,1024]{1,0:T(8,128)(2,1)S(1)}, bf16[1024,1024]{1,0:T(8,128)(2,1)}, u32[]{:S(2)}) copy-start(bf16[1024,1024]{1,0:T(8,128)(2,1)} %basis_ref.1) | copy-start | bytes 6291460
  4.3 1.0 %copy-start.1 = (f32[1024,128]{1,0:T(8,128)S(1)}, f32[1024,128]{1,0:T(8,128)}, u32[]{:S(2)}) copy-start(f32[1024,128]{1,0:T(8,128)} %pad.18.logs_ref) | copy-start | bytes 1572868
  96.0 1.0 %copy-start.2 = (bf16[256,8,128]{2,1,0:T(8,128)(2,1)S(1)}, bf16[256,8,128]{2,1,0:T(8,128)(2,1)}, u32[]{:S(2)}) copy-start(bf16[256,8,128]{2,1,0:T(8,128)(2,1)} %param.6) | copy-start | bytes 1572868

commit v3 on v2

--- a/solution.py
+++ b/solution.py
@@ -15,23 +15,26 @@
 MESH = pl.DeviceIdType.MESH
 
 
-def split_parts(values, pattern):
+def split_parts(values, pattern, axis):
     parts, rest = [], values
     for _ in range(3):
         part = rest.astype(jnp.bfloat16)
         parts.append(part.astype(jnp.float32))
         rest = rest - parts[-1]
-    group = lax.broadcasted_iota(jnp.int32, values.shape, 1) // GROUP
+    group = lax.broadcasted_iota(jnp.int32, values.shape, axis) // GROUP
     chosen = jnp.zeros_like(values)
     for index, which in enumerate(pattern):
         chosen = jnp.where(group == index, parts[which], chosen)
     return chosen.astype(jnp.bfloat16)
 
 
-def spread(columns):
-    padded = jnp.pad(columns, ((0, 0), (0, GROUP - columns.shape[1])))
+def spread(rows):
+    def zeros(count):
+        return jnp.zeros((count, rows.shape[1]), rows.dtype)
+
     copies = len(NODE_PARTS)
-    return jnp.pad(jnp.tile(padded, (1, copies)), ((0, 0), (0, LANES - copies * GROUP)))
+    one = jnp.concatenate([rows, zeros(GROUP - rows.shape[0])], axis=0)
+    return jnp.concatenate([one] * copies + [zeros(LANES - copies * GROUP)], axis=0)
 
 
 def dot_nt(a, b):
@@ -43,9 +46,9 @@
 
 
 def picard_kernel(
-    dims, modes_ref, basis_ref, aux_ref, logs_ref, out_ref,
+    dims, modes_ref, basis_ref, nodes_ref, weights_ref, rates_ref, logs_ref, out_ref,
     basis, first, second, halo_out, field_a, field_b, coeff, faces, weighted, outgoing, landed,
-    local_sem, b_send, b_recv, m_send, m_recv, h_send, h_recv, o_send, o_recv,
+    local_sem, load_sem, b_send, b_recv, m_send, m_recv, h_send, h_recv, o_send, o_recv,
 ):
     n, ny, nx, kl, ql, terms, rows, cols, qb = dims
     modes, cells, rim = n * kl, rows * cols, 2 * rows
@@ -85,16 +88,23 @@
     def peer(step):
         return lax.rem(z + step, n)
 
-    load_basis = pltpu.make_async_copy(
-        basis_ref, basis.at[pl.ds(pl.multiple_of(z * ql, ql), ql), pl.ds(0, modes)], local_sem.at[0]
-    )
-    load_basis.start()
-    for step in range(1, n):
-        remote(modes_copy(peer(step)), modes_slot(z), m_send.at[step], m_recv.at[step], (peer(step), gy, gx)).start()
-    load_modes = pltpu.make_async_copy(modes_copy(z), modes_slot(z), local_sem.at[1])
-    load_modes.start()
-    basis[pl.ds(pl.multiple_of(z * ql, ql), ql), modes : modes + LANES] = split_parts(aux_ref[...], NODE_PARTS)
-    load_basis.wait()
+    place = gy * nx + gx
+    loads = []
+    for step in range(ny * nx):
+        offset = pl.multiple_of(lax.rem(place + step, ny * nx) * piece, piece)
+        loads.append(
+            pltpu.make_async_copy(
+                basis_ref.at[pl.ds(offset, piece), :],
+                basis.at[pl.ds(pl.multiple_of(z * ql + offset, piece), piece), pl.ds(0, modes)],
+                load_sem.at[step],
+            )
+        )
+        loads[-1].start()
+    scalars_rows = jnp.concatenate([nodes_ref[...], weights_ref[...], rates_ref[...]], axis=0)
+    basis[pl.ds(pl.multiple_of(z * ql, ql), ql), modes : modes + LANES] = split_parts(
+        spread(scalars_rows).T, NODE_PARTS, 1
+    )
+    loads[0].wait()
 
     def rows_at(shard, y, x, part=None):
         start = shard * ql + (y * nx + x) * piece
@@ -125,6 +135,11 @@
     @pl.when(z > 0)
     def _():
         down(z).start()
+
+    for step in range(1, n):
+        remote(modes_copy(peer(step)), modes_slot(z), m_send.at[step], m_recv.at[step], (peer(step), gy, gx)).start()
+    load_modes = pltpu.make_async_copy(modes_copy(z), modes_slot(z), local_sem.at[0])
+    load_modes.start()
 
     def plane(shard):
         mine = rows_at(shard, gy, gx)
@@ -311,13 +326,16 @@
     per_shard = ql // qb
     fields = (field_a, field_b)
 
-    def drive_shard(shard):
+    def drive_shard(shard, between):
         base = shard * per_shard
         multiply(fields[0], base, first)
         for i in range(per_shard):
             if i + 1 < per_shard:
                 multiply(fields[(i + 1) % 2], base + i + 1, first)
             drive(fields[i % 2], base + i, True)
+            if i == 0:
+                for call in between:
+                    call()
 
     def drive_all():
         count = n * per_shard
@@ -332,15 +350,14 @@
         multiply(field_a, 0, second)
         lax.fori_loop(0, count // 2, pair, 0)
 
-    first[own, modes : modes + LANES] = split_parts(
-        logs_ref[pl.ds(pl.multiple_of(block * cells, cells), cells), :], LOG_PARTS
-    )
-    load_modes.wait()
-    for step in range(1, n):
-        source = lax.rem(z - step + n, n)
-        remote(modes_slot(source), modes_slot(source), m_send.at[step], m_recv.at[step], to_y).wait_recv()
+    cell_at = lax.broadcasted_iota(jnp.int32, (cells, logs_ref.shape[2]), 0)
+    x_at = lax.broadcasted_iota(jnp.int32, (cells, logs_ref.shape[2]), 1) - block * cols
+    logs = jnp.zeros((cells, LANES), jnp.float32)
+    for y in range(rows):
+        take = (cell_at == x_at * rows + y).astype(jnp.float32).astype(jnp.bfloat16)
+        logs += dot_nt(take, split_parts(spread(logs_ref[:, y, :]), LOG_PARTS, 0))
+    first[own, modes : modes + LANES] = logs.astype(jnp.bfloat16)
     halo_a = halo(0, first)
-    halo_a[0]()
 
     def nth(j):
         shard = jnp.int32(0)
@@ -351,18 +368,31 @@
 
     shards = [nth(j) for j in range(n - 1)]
     stages = (stage_z, stage_xy, stage_d)
-    stage_z(shards[0])
+
+    def turn_stages(turn):
+        calls = []
+        for depth, stage in reversed(list(enumerate(stages))):
+            if 0 <= turn - depth < n - 1:
+                calls.append(functools.partial(stage, shards[turn - depth]))
+        return calls
+
+    for call in turn_stages(0) + turn_stages(1):
+        call()
+    for load in loads[1:]:
+        load.wait()
+    load_modes.wait()
+    for step in range(1, n):
+        source = lax.rem(z - step + n, n)
+        remote(modes_slot(source), modes_slot(source), m_send.at[step], m_recv.at[step], to_y).wait_recv()
+    halo_a[0]()
+    early = turn_stages(2)
+    for call in early[:-1]:
+        call()
     halo_a[1]()
-    drive_shard(z)
-    for turn in range(1, n + 1):
-        for depth, stage in reversed(list(enumerate(stages))):
-            j = turn - depth
-            if 0 <= j < n - 1 and (j, depth) != (0, 0):
-                stage(shards[j])
-        j = turn - 2
-        if 0 <= j < n - 1:
-            stage_s(shards[j])
-            drive_shard(shards[j])
+    drive_shard(z, early[-1:])
+    for j in range(n - 1):
+        stage_s(shards[j])
+        drive_shard(shards[j], turn_stages(j + 3))
 
     def project(rank):
         span = pl.ds(pl.multiple_of(rank * kl, kl), kl)
@@ -426,8 +456,6 @@
     ext = modes + LANES
     dims = (n, ny, nx, kl, ql, terms, rows, cols, qb)
     modes_t = modes_now.transpose(2, 1, 0).reshape(tile, kl)
-    aux = spread(jnp.concatenate([germ_nodes, quad_weights[:, None], reaction_rates[:, None]], axis=1))
-    logs = spread(log_fields.transpose(2, 1, 0).reshape(tile, terms))
     any_spec, vmem = pl.BlockSpec(memory_space=pl.ANY), pl.BlockSpec(memory_space=pltpu.VMEM)
     grid_rows = 2 * rim + cells + 2 * cols
     bf16, f32 = jnp.bfloat16, jnp.float32
@@ -435,7 +463,7 @@
     delta_t = pl.pallas_call(
         functools.partial(picard_kernel, dims),
         out_shape=jax.ShapeDtypeStruct((tile, kl), bf16),
-        in_specs=[any_spec, any_spec, vmem, vmem],
+        in_specs=[any_spec, any_spec, vmem, vmem, vmem, vmem],
         out_specs=vmem,
         scratch_shapes=[
             pltpu.VMEM((quad_pts, ext), bf16),
@@ -449,7 +477,8 @@
             pltpu.VMEM((cells, quad_pts), bf16),
             pltpu.VMEM((n, cells, kl), bf16),
             pltpu.VMEM((tile, kl), bf16),
-            dma((2,)),
+            dma((1,)),
+            dma((ny * nx,)),
             dma((n, 11)),
             dma((n, 11)),
             dma((n,)),
@@ -462,7 +491,7 @@
         compiler_params=pltpu.CompilerParams(
             collective_id=0, has_side_effects=True, vmem_limit_bytes=48 * 1024 * 1024
         ),
-    )(modes_t, basis_rows, aux, logs)
+    )(modes_t, basis_rows, germ_nodes.T, quad_weights[None], reaction_rates[None], log_fields)
     delta = delta_t.reshape(width, rows, kl).transpose(2, 1, 0)
     return modes_now.astype(f32) + time_step * delta.astype(f32)
 

time: 98.4 us -> 92.5 us (0.940)
  Pallas kernels: 90.7 us -> 83.1 us
  local copies, waits for them, and re-layouts: 5.36 us -> 6.99 us
    pallas_call x1, Pallas kernels: 90.7 us -> 83.1 us  [fast_body(): pl.pallas_call(functools.partial(picard_kernel, dims), out_shape=jax.Shap...]
    unnamed x8 -> x12, local copies, waits for them, and re-layouts: 1.41 us -> 4.84 us
where the time goes in v3:
time: 92.5 us; the launch traced here: 91.3 us
  Pallas kernels  83.1 us (90%)
  local copies, waits for them, and re-layouts  6.99 us (8%)
  other arithmetic  1.15 us (1%)
    pallas_call x1, Pallas kernels, fast_body(): pl.pallas_call(functools.partial(picard_kernel, dims), out_shape=jax.Shap...  83.1 us
    unnamed x12, local copies, waits for them, and re-layouts  4.84 us

profile of v3, /device:TPU:9, one launch (start us, length us, event | category | flops | bytes accessed | tf_op | source)
XLA Modules:
  0.0 91.3 jit_solution(4804422178956420179)
XLA Ops:
  0.0 1.6 %copy.7 = bf16[128,8,256]{2,1,0:T(8,128)(2,1)S(1)} copy(bf16[128,8,256]{0,1,2:T(8,128)(2,1)} %bitcast.13) | data formatting | bytes 1048576 | tf_op jit(solution)/shard_map/transpose | solution.py:458
  1.6 0.0 copy-start
  1.6 1.6 %copy-done = bf16[1024,1024]{1,0:T(8,128)(2,1)S(1)} copy-done((bf16[1024,1024]{1,0:T(8,128)(2,1)S(1)}, bf16[1024,1024]{1,0:T(8,128)(2,1)}, u32[]{:S(2)}) %copy-start) | copy-done | bytes 2097176
  3.2 0.0 copy-start.1
  3.2 0.8 copy-done.1
  4.0 0.0 copy-start.2
  4.0 0.8 copy-done.2
  4.7 0.0 copy-start.3
  4.7 0.7 copy-done.3
  5.4 0.0 copy-start.4
  5.4 0.7 copy-done.4
  6.1 83.1 %shard_map.64 = bf16[1024,256]{1,0:T(8,128)(2,1)S(1)} custom-call(bf16[1024,256]{1,0:T(8,128)(2,1)S(1)} %bitcast.9, bf16[1024,1024]{1,0:T(8,128)(2,1)S(1)} %copy-done, f32[8,1024]{1,0:T(8,128)S(1)} %bitcast.10, f32[1,1024]{1,0:T(1,128)S(1)} %bitcast.11, f32[1,1024]{1,0:T(1,128)S(1)} %bitcast.12, f32[8,8,128]{2,1,0:T(8,128)S(1)} %copy-done.2), custom_call_target="tpu_custom_call" | custom-call | tf_op jit(solution)/shard_map/pallas_call | solution.py:463
  89.2 0.0 copy-start.5
  89.2 0.1 multiply_bitcast_fusion
  89.3 0.6 copy.8
  89.9 0.4 copy-done.5
  90.2 1.1 %bitcast_add_fusion = f32[256,8,128]{2,1,0:T(8,128)} fusion(f32[128,8,256]{0,1,2:T(8,128)S(1)} %copy.8, bf16[256,8,128]{2,1,0:T(8,128)(2,1)S(1)} %copy-done.5), kind=kLoop, calls=%fused_computation | loop fusion | flops 524288 | bytes 2621440 | tf_op jit(solution)/shard_map/add | solution.py:496
Async XLA Ops:
  1.6 1.6 %copy-start = (bf16[1024,1024]{1,0:T(8,128)(2,1)S(1)}, bf16[1024,1024]{1,0:T(8,128)(2,1)}, u32[]{:S(2)}) copy-start(bf16[1024,1024]{1,0:T(8,128)(2,1)} %basis_ref.1) | copy-start | bytes 6291460
  3.2 0.8 copy-start.1
  4.0 0.8 copy-start.2
  4.7 0.7 copy-start.3
  5.4 0.7 copy-start.4
  89.2 1.0 %copy-start.5 = (bf16[256,8,128]{2,1,0:T(8,128)(2,1)S(1)}, bf16[256,8,128]{2,1,0:T(8,128)(2,1)}, u32[]{:S(2)}) copy-start(bf16[256,8,128]{2,1,0:T(8,128)(2,1)} %param.6) | copy-start | bytes 1572868

commit v4 on v3

--- a/solution.py
+++ b/solution.py
@@ -113,7 +113,8 @@
         half = piece // 2
         return basis.at[pl.ds(pl.multiple_of(start + part * half, half), half), :]
 
-    Z, X, Y, DA, DB, S0, SX, SY, SA, SB, ZB = range(11)
+    Z, X, Y, ZB = (0, 1), (2, 3), (4, 5), (6, 7)
+    DA, DB, S0, SX, SY, SA, SB = range(8, 15)
 
     def push(ref, shard, kind, target, send_kind=None):
         send_kind = kind if send_kind is None else send_kind
@@ -122,28 +123,35 @@
     def arrived(ref, shard, kind):
         push(ref, shard, kind, to_core).wait_recv()
 
-    def up(shard):
-        return push(rows_at(shard, gy, gx), shard, Z, (jnp.minimum(z + 1, n - 1), gy, gx))
-
-    def down(shard):
-        return push(rows_at(shard, gy, gx), shard, Z, (jnp.maximum(z - 1, 0), gy, gx), ZB)
+    def up(shard, part):
+        target = (jnp.minimum(z + 1, n - 1), gy, gx)
+        return push(rows_at(shard, gy, gx, part), shard, Z[part], target)
+
+    def down(shard, part):
+        target = (jnp.maximum(z - 1, 0), gy, gx)
+        return push(rows_at(shard, gy, gx, part), shard, Z[part], target, ZB[part])
 
     @pl.when(z < n - 1)
     def _():
-        up(z).start()
+        for part in (0, 1):
+            up(z, part).start()
 
     @pl.when(z > 0)
     def _():
-        down(z).start()
+        for part in (0, 1):
+            down(z, part).start()
 
     for step in range(1, n):
         remote(modes_copy(peer(step)), modes_slot(z), m_send.at[step], m_recv.at[step], (peer(step), gy, gx)).start()
     load_modes = pltpu.make_async_copy(modes_copy(z), modes_slot(z), local_sem.at[0])
     load_modes.start()
 
-    def plane(shard):
-        mine = rows_at(shard, gy, gx)
-        return [push(mine, shard, X, to_x), push(mine, shard, Y, to_y), push(mine, shard, S0, to_core)]
+    def plane(shard, part):
+        mine = rows_at(shard, gy, gx, part)
+        return [push(mine, shard, X[part], to_x), push(mine, shard, Y[part], to_y)]
+
+    def to_sibling(shard):
+        return push(rows_at(shard, gy, gx), shard, S0, to_core)
 
     def relay(shard):
         by_x, by_y = rows_at(shard, gy, other_x), rows_at(shard, other_gy, gx)
@@ -159,24 +167,29 @@
         ]
 
     def stage_z(shard):
-        arrived(rows_at(shard, gy, gx), shard, Z)
-        for copy in plane(shard):
-            copy.start()
-
-        @pl.when((shard < z) & (z < n - 1))
-        def _():
-            up(shard).start()
-
-        @pl.when((shard > z) & (z > 0))
-        def _():
-            down(shard).start()
+        for part in (0, 1):
+            arrived(rows_at(shard, gy, gx, part), shard, Z[part])
+
+            @pl.when((shard < z) & (z < n - 1))
+            def _():
+                up(shard, part).start()
+
+            @pl.when((shard > z) & (z > 0))
+            def _():
+                down(shard, part).start()
+
+            for copy in plane(shard, part):
+                copy.start()
+        to_sibling(shard).start()
 
     def stage_xy(shard):
         after_x, after_y = relay(shard)
-        arrived(rows_at(shard, gy, other_x), shard, X)
-        for copy in after_x:
-            copy.start()
-        arrived(rows_at(shard, other_gy, gx), shard, Y)
+        arrived(rows_at(shard, gy, other_x, 0), shard, X[0])
+        after_x[0].start()
+        arrived(rows_at(shard, gy, other_x, 1), shard, X[1])
+        after_x[1].start()
+        arrived(rows_at(shard, other_gy, gx, 0), shard, Y[0])
+        arrived(rows_at(shard, other_gy, gx, 1), shard, Y[1])
         for copy in after_y:
             copy.start()
 
@@ -196,16 +209,18 @@
         arrived(rows_at(shard, other_gy, core_x, 1), shard, SB)
 
     def drain(shard):
-        for copy in plane(shard) + relay(shard)[0] + relay(shard)[1] + across(shard):
+        copies = plane(shard, 0) + plane(shard, 1) + [to_sibling(shard)]
+        for copy in copies + relay(shard)[0] + relay(shard)[1] + across(shard):
             copy.wait_send()
-
-        @pl.when((shard < z) & (z < n - 1))
-        def _():
-            up(shard).wait_send()
-
-        @pl.when((shard > z) & (z > 0))
-        def _():
-            down(shard).wait_send()
+        for part in (0, 1):
+
+            @pl.when((shard < z) & (z < n - 1))
+            def _():
+                up(shard, part).wait_send()
+
+            @pl.when((shard > z) & (z > 0))
+            def _():
+                down(shard, part).wait_send()
 
     block = block_of(z)
     ahead = jnp.where(even, 1, -1)
@@ -434,13 +449,15 @@
     halo_a[2]()
     halo_b[2]()
 
-    @pl.when(z < n - 1)
-    def _():
-        up(z).wait_send()
-
-    @pl.when(z > 0)
-    def _():
-        down(z).wait_send()
+    for part in (0, 1):
+
+        @pl.when(z < n - 1)
+        def _():
+            up(z, part).wait_send()
+
+        @pl.when(z > 0)
+        def _():
+            down(z, part).wait_send()
 
     for shard in shards:
         drain(shard)
@@ -479,8 +496,8 @@
             pltpu.VMEM((tile, kl), bf16),
             dma((1,)),
             dma((ny * nx,)),
-            dma((n, 11)),
-            dma((n, 11)),
+            dma((n, 15)),
+            dma((n, 15)),
             dma((n,)),
             dma((n,)),
             dma((2, 4)),

time: 92.5 us -> 91.5 us (0.989)
  no operation moved by 1% of the time
where the time goes in v4:
time: 91.5 us; the launch traced here: 91 us
  Pallas kernels  82.8 us (90%)
  local copies, waits for them, and re-layouts  6.99 us (8%)
  other arithmetic  1.15 us (1%)
    pallas_call x1, Pallas kernels, fast_body(): pl.pallas_call(functools.partial(picard_kernel, dims), out_shape=jax.Shap...  82.8 us
    unnamed x12, local copies, waits for them, and re-layouts  4.84 us

profile of v4, /device:TPU:9, one launch (start us, length us, event | category | flops | bytes accessed | tf_op | source)
XLA Modules:
  0.0 91.0 jit_solution(11474295043064532332)
XLA Ops:
  0.0 1.6 %copy.7 = bf16[128,8,256]{2,1,0:T(8,128)(2,1)S(1)} copy(bf16[128,8,256]{0,1,2:T(8,128)(2,1)} %bitcast.13) | data formatting | bytes 1048576 | tf_op jit(solution)/shard_map/transpose | solution.py:475
  1.6 0.0 copy-start
  1.6 1.6 %copy-done = bf16[1024,1024]{1,0:T(8,128)(2,1)S(1)} copy-done((bf16[1024,1024]{1,0:T(8,128)(2,1)S(1)}, bf16[1024,1024]{1,0:T(8,128)(2,1)}, u32[]{:S(2)}) %copy-start) | copy-done | bytes 2097176
  3.2 0.0 copy-start.1
  3.2 0.8 copy-done.1
  4.0 0.0 copy-start.2
  4.0 0.8 copy-done.2
  4.7 0.0 copy-start.3
  4.7 0.7 copy-done.3
  5.4 0.0 copy-start.4
  5.4 0.7 copy-done.4
  6.1 82.8 %shard_map.64 = bf16[1024,256]{1,0:T(8,128)(2,1)S(1)} custom-call(bf16[1024,256]{1,0:T(8,128)(2,1)S(1)} %bitcast.9, bf16[1024,1024]{1,0:T(8,128)(2,1)S(1)} %copy-done, f32[8,1024]{1,0:T(8,128)S(1)} %bitcast.10, f32[1,1024]{1,0:T(1,128)S(1)} %bitcast.11, f32[1,1024]{1,0:T(1,128)S(1)} %bitcast.12, f32[8,8,128]{2,1,0:T(8,128)S(1)} %copy-done.2), custom_call_target="tpu_custom_call" | custom-call | tf_op jit(solution)/shard_map/pallas_call | solution.py:480
  88.9 0.0 copy-start.5
  88.9 0.1 multiply_bitcast_fusion
  89.0 0.6 copy.8
  89.6 0.4 copy-done.5
  90.0 1.1 %bitcast_add_fusion = f32[256,8,128]{2,1,0:T(8,128)} fusion(f32[128,8,256]{0,1,2:T(8,128)S(1)} %copy.8, bf16[256,8,128]{2,1,0:T(8,128)(2,1)S(1)} %copy-done.5), kind=kLoop, calls=%fused_computation | loop fusion | flops 524288 | bytes 2621440 | tf_op jit(solution)/shard_map/add | solution.py:513
Async XLA Ops:
  1.6 1.6 %copy-start = (bf16[1024,1024]{1,0:T(8,128)(2,1)S(1)}, bf16[1024,1024]{1,0:T(8,128)(2,1)}, u32[]{:S(2)}) copy-start(bf16[1024,1024]{1,0:T(8,128)(2,1)} %basis_ref.1) | copy-start | bytes 6291460
  3.2 0.8 copy-start.1
  4.0 0.8 copy-start.2
  4.7 0.7 copy-start.3
  5.4 0.7 copy-start.4
  88.9 1.0 %copy-start.5 = (bf16[256,8,128]{2,1,0:T(8,128)(2,1)S(1)}, bf16[256,8,128]{2,1,0:T(8,128)(2,1)}, u32[]{:S(2)}) copy-start(bf16[256,8,128]{2,1,0:T(8,128)(2,1)} %param.6) | copy-start | bytes 1572868
